TPU v7x, 128 devices: a whole 4x4x4 slice. The times are simulated.
128 devices in a mesh: row: 32 (over z, y, x_hi), col: 4 (over x_lo, core).
Axes of the slice: x: 4 (x_hi: 2, x_lo: 2; x = x_hi * 2 + x_lo), y: 4, z: 4, core: 2. Of those that a mesh axis runs over, the one named last changes fastest.
Arguments:
- source: bfloat16 [64, 32768], P(None, ('row', 'col')), may hold values from -1 to 1
- target: bfloat16 [64, 98304], P(None, ('col', 'row')), may hold values from -1 to 1
- source_logw: float32 [32768], P('row'), may hold values from -3 to 0
- target_logw: float32 [98304], P(('col', 'row')), may hold values from -3 to 0
- start_potential: bfloat16 [1, 98304], P(None, ('col', 'row')), may hold values from -1 to 12
Outputs:
- row_potential: float32 [32768], P('row')
- col_potential: float32 [98304], P(('col', 'row'))
All inputs are finite; a program needn't handle non-finite values.
Results may differ from a plain program's by a relative error of at most 0.0015.
Values may be sent and summed in bfloat16 or wider, within the bound.
No kernel may reach another device: no remote copies, remote signals or barrier semaphores. Data moves between devices by JAX's collectives and lax.ppermute only.
A program may use at most 64 MiB of HBM per device.

v0:
```python
import math

import jax
import jax.numpy as jnp
from jax import lax
from jax.sharding import PartitionSpec as P

smoothing = 0.1
floor_value = -1e30


def combined_all(part, axis, combine):
    gathered = jax.tree.map(lambda a: lax.all_gather(a, axis), part)

    def take(source):
        return jax.tree.map(lambda a: lax.dynamic_index_in_dim(a, source, 0, False), gathered)

    return lax.fori_loop(
        1, lax.axis_size(axis), lambda source, state: combine(state, take(source)), take(0)
    )


def column_norms(points):
    wide = points.astype(jnp.float32)
    return jnp.sum(wide * wide, axis=0)


def cost_block(rows, row_sq, cols, col_sq):
    inner = lax.dot_general(
        rows, cols, (((0,), (0,)), ((), ())), preferred_element_type=jnp.float32
    )
    return row_sq[:, None] + col_sq[None, :] - 2.0 * inner


def fold_lse(first, second):
    top = jnp.maximum(first[0], second[0])
    return (top, first[1] * jnp.exp(first[0] - top) + second[1] * jnp.exp(second[0] - top))


def row_terms(rows, row_sq, cols, lifted):
    width = math.gcd(cols.shape[1], 2048)

    def row_step(carry, index):
        piece = lax.dynamic_slice_in_dim(cols, index * width, width, 1)
        lift = lax.dynamic_slice_in_dim(lifted, index * width, width, 1)
        scores = (
            lift.astype(jnp.float32) - cost_block(rows, row_sq, piece, column_norms(piece))
        ) / smoothing
        top = jnp.max(scores, axis=1)
        return (fold_lse(carry, (top, jnp.sum(jnp.exp(scores - top[:, None]), axis=1))), None)

    count = rows.shape[1]
    start = (jnp.full((count,), floor_value, jnp.float32), jnp.zeros((count,), jnp.float32))
    result, _ = lax.scan(row_step, start, jnp.arange(cols.shape[1] // width, dtype=jnp.int32))
    return result


def column_terms(rows, row_sq, pots, cols):
    width = math.gcd(cols.shape[1], 2048)

    def column_step(index):
        piece = lax.dynamic_slice_in_dim(cols, index * width, width, 1)
        scores = (pots[:, None] - cost_block(rows, row_sq, piece, column_norms(piece))) / smoothing
        top = jnp.max(scores, axis=0)
        return (top, jnp.sum(jnp.exp(scores - top[None, :]), axis=0))

    tops, sums = lax.map(column_step, jnp.arange(cols.shape[1] // width, dtype=jnp.int32))
    return (tops.reshape(cols.shape[1]), sums.reshape(cols.shape[1]))


def per_device(source, target, source_logw, target_logw, start_potential):
    rows = lax.all_gather(source, "col", axis=1, tiled=True)
    row_sq = column_norms(rows)
    count = rows.shape[1]
    tgt_dev = target.shape[1]
    groups = lax.axis_size("row")
    span = tgt_dev * groups
    empty_top = jnp.full((count,), floor_value, jnp.float32)
    empty_sum = jnp.zeros((count,), jnp.float32)
    top, total = fold_lse(
        (empty_top, empty_sum),
        row_terms(
            rows,
            row_sq,
            lax.all_gather(target, "row", axis=1, tiled=True),
            lax.all_gather(start_potential, "row", axis=1, tiled=True),
        ),
    )
    top, total = combined_all((top, total), "col", fold_lse)
    row_potential = smoothing * source_logw - smoothing * (top + jnp.log(total))
    blank = jnp.zeros((span,), jnp.float32)
    start = jnp.int32(0)
    piece_top, piece_sum = column_terms(
        rows, row_sq, row_potential, lax.all_gather(target, "row", axis=1, tiled=True)
    )
    col_top = lax.dynamic_update_slice_in_dim(blank, piece_top, start, 0)
    col_sum = lax.dynamic_update_slice_in_dim(blank, piece_sum, start, 0)
    offset = lax.axis_index("row") * tgt_dev
    whole_top, whole_sum = combined_all((col_top, col_sum), "row", fold_lse)
    own_top = lax.dynamic_slice_in_dim(whole_top, offset, tgt_dev, 0)
    own_sum = lax.dynamic_slice_in_dim(whole_sum, offset, tgt_dev, 0)
    col_total = own_top + jnp.log(own_sum)
    col_potential = smoothing * target_logw - smoothing * col_total
    return (row_potential, col_potential)


def solution(mesh):
    in_specs = (
        P(None, ("row", "col")),
        P(None, ("col", "row")),
        P("row"),
        P(("col", "row")),
        P(None, ("col", "row")),
    )
    out_specs = (P("row"), P(("col", "row")))
    return jax.shard_map(
        per_device, mesh=mesh, in_specs=in_specs, out_specs=out_specs, check_vma=False
    )
```

profile of v0, /device:TPU:8, one launch (start us, length us, event | category | flops | bytes accessed | tf_op | source)
XLA Modules:
  0.0 534.0 jit_solution(5563517432931060098)
XLA Ops:
  8.0 93.3 %all_gather.28 = bf16[1,24576]{1,0:T(2,128)(2,1)S(1)} all-gather(bf16[1,768]{1,0:T(2,128)(2,1)} %param.17), channel_id=1, replica_groups=mesh['row'=32,'col'=4] {'row'}, dimensions={1}, use_global_device_ids=true | all-gather | bytes 50688 | tf_op jit(solution)/shard_map/all_gather | solution.py:86
  101.3 5.6 %all_gather.29 = bf16[64,1024]{1,0:T(8,128)(2,1)S(1)} all-gather(bf16[64,256]{1,0:T(8,128)(2,1)} %param.13), channel_id=1, replica_groups=mesh['row'=32,'col'=4] {'col'}, dimensions={1}, use_global_device_ids=true | all-gather | bytes 163840 | tf_op jit(solution)/shard_map/all_gather | solution.py:72
  107.0 97.5 %while.62 = (s32[]{:T(128)}, f32[1024]{0:T(1024)S(1)}, f32[1024]{0:T(1024)S(1)}, s32[12]{0:T(128)S(1)}, bf16[1,24576]{1,0:T(2,128)(2,1)S(1)}, /*index=5*/f32[102...) while((s32[]{:T(128)}, f32[1024]{0:T(1024)S(1)}, ...), condition=%wide.region_5.6_spmd.clone, body=%wide.region_1.5_spmd.clone.sunk | while | flops 296097792 | bytes 17531084 | solution.py:54
  109.4 3.0 fusion.23
  112.5 2.6 exponential_reduce_fusion.5
  117.5 3.0 fusion.23
  125.7 3.1 fusion.23
  133.8 3.0 fusion.23
  141.9 3.0 fusion.23
  150.0 3.1 fusion.23
  158.2 3.0 fusion.23
  166.3 3.0 fusion.23
  174.4 3.1 fusion.23
  182.6 3.0 fusion.23
  190.7 3.0 fusion.23
  198.8 3.1 fusion.23
  204.6 5.2 all-gather.1
  209.8 5.2 all-gather
  215.2 111.0 %while.60 = (s32[]{:T(128)}, f32[12,2048]{1,0:T(8,128)S(1)}, f32[12,2048]{1,0:T(8,128)S(1)}, f32[1024]{0:T(1024)S(1)}, f32[1024]{0:T(1024)S(1)}, /*index=5*/s32[...) while((s32[]{:T(128)}, f32[12,2048]{1,0:T(8,128)S(1)}, ...), condition=%wide.region_12.13_spmd, body=%wide.region_8.12_spmd.sunk | while | flops 296085504 | bytes 17531080 | solution.py:67
  217.4 3.1 fusion.21
  220.5 3.4 exponential_reduce_fusion.4
  226.7 3.1 fusion.21
  229.8 3.4 exponential_reduce_fusion.4
  235.9 3.1 fusion.21
  239.0 3.4 exponential_reduce_fusion.4
  245.2 3.1 fusion.21
  248.3 3.4 exponential_reduce_fusion.4
  254.4 3.1 fusion.21
  257.5 3.4 exponential_reduce_fusion.4
  263.7 3.1 fusion.21
  266.8 3.4 exponential_reduce_fusion.4
  272.9 3.1 fusion.21
  276.0 3.4 exponential_reduce_fusion.4
  282.2 3.1 fusion.21
  285.3 3.4 exponential_reduce_fusion.4
  291.4 3.1 fusion.21
  294.5 3.4 exponential_reduce_fusion.4
  300.7 3.1 fusion.21
  303.8 3.4 exponential_reduce_fusion.4
  309.9 3.1 fusion.21
  313.0 3.4 exponential_reduce_fusion.4
  319.2 3.1 fusion.21
  322.3 3.4 exponential_reduce_fusion.4
  328.0 72.2 %all-gather.12.cloned.1.call-done = f32[32,1,24576]{2,1,0:T(1,128)} async-done(((f32[1,1,24576]{2,1,0:T(1,128)}), f32[32,1,24576]{2,1,0:T(1,128)}) %all-gather.12.cloned.1.call-update) | async-done | bytes 3145744 | tf_op jit(solution)/shard_map/all_gather | solution.py:13
  400.1 3.8 copy.11
  403.9 73.3 %all-gather.10.cloned.1.call-done = f32[32,1,24576]{2,1,0:T(1,128)} async-done(((f32[1,1,24576]{2,1,0:T(1,128)}), f32[32,1,24576]{2,1,0:T(1,128)}) %all-gather.10.cloned.1.call-update) | async-done | bytes 3145744 | tf_op jit(solution)/shard_map/all_gather | solution.py:13
  478.1 5.4 %copy.12 = f32[32,1,24576]{2,0,1:T(8,128)} copy(f32[32,1,24576]{2,1,0:T(1,128)} %all-gather.10.cloned.1.call-done) | data formatting | bytes 6291456
  483.5 43.2 %while.61 = (s32[]{:T(128)}, f32[24576]{0:T(1024)S(1)}, f32[24576]{0:T(1024)S(1)}, f32[32,24576]{1,0:T(8,128)}, f32[32,24576]{1,0:T(8,128)S(1)}, /*index=5*/s32[]{:T(128)}, s32[]{:T(128)}, s32[]{:T(128)}) while((s32[]{:T(128)}, f32[24576]{0:T(1024)S(1)}, f32[24576]{0:T(1024)S(1)}, f32[32,24576]{1,0:T(8,128)}, f32[32,24576]{1,0:T(8,128)S(1)}, ...), condition=%wide.region_14.15_spmd, body=%wide.region_13.14_spmd.sunk | while | flops 147461 | bytes 983163 | solution.py:18
  (208 shorter events, 120.7 us)
Async XLA Ops:
  7.2 99.8 %all-gather.8.cloned.1.call-start = ((), (), s32[]{:S(2)}) async-start(), calls=%async_computation | async-start | bytes 3244032 | tf_op jit(solution)/shard_map/all_gather | solution.py:85
  7.9 392.2 %all-gather.12.cloned.1.call-start = ((), (), s32[]{:S(2)}) async-start(), calls=%async_computation.2 | async-start | bytes 3244032 | tf_op jit(solution)/shard_map/all_gather | solution.py:13
  107.0 108.2 %copy-start.1 = (f32[1024]{0:T(1024)S(1)}, f32[1024]{0:T(1024)}, u32[]{:S(2)}) copy-start(f32[1024]{0:T(1024)} %param.15) | copy-start | bytes 12292
  326.2 157.4 %copy-start = (f32[1024]{0:T(1024)}, f32[1024]{0:T(1024)S(1)}, u32[]{:S(2)}) copy-start(f32[1024]{0:T(1024)S(1)} %get-tuple-element.778) | copy-start | bytes 12292
  326.9 150.3 %all-gather.10.cloned.1.call-start = ((), (), s32[]{:S(2)}) async-start(), calls=%async_computation.1 | async-start | bytes 3244032 | tf_op jit(solution)/shard_map/all_gather | solution.py:13
  400.1 83.4 %slice-start = ((f32[32,1,24576]{2,1,0:T(1,128)}), f32[1,1,24576]{2,1,0:T(1,128)S(1)}, s32[]{:S(2)}) async-start(f32[32,1,24576]{2,1,0:T(1,128)} %all-gather.12.cloned.1.call-done), calls=%async_computation.3 | async-start | bytes 196608 | tf_op jit(solution)/shard_map/jit(dynamic_index_in_dim)/dynamic_slice | solution.py:16
  400.1 126.6 %copy-start.2 = (f32[768]{0:T(1024)S(1)}, f32[768]{0:T(1024)}, u32[]{:S(2)}) copy-start(f32[768]{0:T(1024)} %param.16) | copy-start | bytes 9220
Sparse Core Ops, SparseCore 0:
  10.8 79.8 all-gather.7
  327.1 73.0 all-gather.11
  403.1 74.0 all-gather.9
where the time goes:
time: 538 us; the launch traced here: 534 us
  waiting for transfers between devices  146 us (27%)
  blocking collectives  109 us (20%)
  other arithmetic  101 us (19%)
  matrix products  73.6 us (14%)
  local copies, waits for them, and re-layouts  71.1 us (13%)
  loops' own time  18.1 us (3%)
  between operations  13.9 us (3%)
    all_gather x2, waiting for transfers between devices, combined_all(): gathered = jax.tree.map(lambda a: lax.all_gather(a, axis), part)  145 us
    all_gather x1, blocking collectives, per_device(): lax.all_gather(start_potential, 'row', axis=1, tiled=True)  93.3 us
    dot_general x24, matrix products, cost_block(): lax.dot_general(rows, cols, (((0,), (0,)), ((), ())), preferred_element_t...  73.6 us
    reduce_sum x12, other arithmetic, column_step(): return (top, jnp.sum(jnp.exp(scores - top[None, :]), axis=0))  41.3 us
    dynamic_slice x39, local copies, waits for them, and re-layouts, take(): lax.dynamic_index_in_dim(a, source, 0, False)  40.5 us
    reduce_sum x12, other arithmetic, row_step(): jnp.sum(jnp.exp(scores - top[:, None]), axis=1)  31.6 us
    reduce_sum x25, other arithmetic, column_norms(): return jnp.sum(wide * wide, axis=0)  24.6 us
    dynamic_slice x24, local copies, waits for them, and re-layouts, row_terms(): lax.scan(row_step, start, jnp.arange(cols.shape[1] // width, dtype=jnp.in...  15 us
  transfers between devices with their start and end apart: 3, of which 2 were waited for; matrix products, arithmetic and copies ran while one was open for 1% of the time, Pallas kernels for 0%

commit v1 on v0

v1 whole, which is shorter than its diff:
```python
import functools
import math

import jax
import jax.numpy as jnp
from jax import lax
from jax.experimental import pallas as pl
from jax.experimental.pallas import tpu as pltpu
from jax.sharding import Mesh
from jax.sharding import PartitionSpec as P

smoothing = 0.1
log2e = math.log2(math.e)
kappa = 2.0 * log2e / smoothing
scale = log2e / smoothing
dim = 64
headroom = 56.0
largest = 3e38
shape = (4, 4, 2, 2, 2)
names = ("z", "y", "xh", "xl", "core")


def three_parts(x):
    hi = x.astype(jnp.bfloat16).astype(jnp.float32)
    mid = (x - hi).astype(jnp.bfloat16).astype(jnp.float32)
    return hi, mid, x - hi - mid


def streamed_features(points, bias):
    m = points.shape[1]
    hi, mid, lo = three_parts(bias)
    row = lax.broadcasted_iota(jnp.int32, (16, m), 0)
    extra = jnp.where(row == 0, hi, jnp.where(row == 1, mid, jnp.where(row == 2, lo, 0.0)))
    extra = jnp.where(row == 3, 1.0, extra).astype(jnp.bfloat16)
    block = jnp.concatenate([points, extra, jnp.zeros((48, m), jnp.bfloat16)], axis=0)
    return block.T


def held_features(points, shift):
    n = points.shape[1]
    wide = points.astype(jnp.float32) * kappa
    hi = wide.astype(jnp.bfloat16)
    lo = (wide - hi.astype(jnp.float32)).astype(jnp.bfloat16)
    row = lax.broadcasted_iota(jnp.int32, (16, n), 0)
    extra = jnp.where(row < 3, 1.0, jnp.where(row == 3, -shift, 0.0)).astype(jnp.bfloat16)
    return jnp.concatenate(
        [hi, extra, jnp.zeros((48, n), jnp.bfloat16), lo, jnp.zeros((64, n), jnp.bfloat16)], axis=0
    )


def scores(stream_ref, start, size, held):
    u = stream_ref[pl.ds(start, size), :]
    return lax.dot_general(
        jnp.concatenate([u, u], axis=1),
        held,
        (((1,), (0,)), ((), ())),
        preferred_element_type=jnp.float32,
    )


def log_sums(stream_ref, points, chunk, unroll, sample=128):
    m, n = stream_ref.shape[0], points.shape[1]

    def start_of(c):
        return pl.multiple_of(c * chunk, chunk)

    def total(shift):
        held = held_features(points, shift)

        def step(c, acc):
            e = jnp.exp2(scores(stream_ref, start_of(c), chunk, held))
            return acc + jnp.sum(e.reshape(chunk // 8, 8, n), axis=0)

        acc = lax.fori_loop(0, m // chunk, step, jnp.zeros((8, n), jnp.float32), unroll=unroll)
        return jnp.sum(acc, axis=0, keepdims=True)

    def rounded(x):
        return x.astype(jnp.bfloat16).astype(jnp.float32)

    bare = held_features(points, jnp.zeros((1, n), jnp.float32))
    top = jnp.max(scores(stream_ref, 0, sample, bare), axis=0, keepdims=True)
    shift = rounded(top + headroom)
    sums = total(shift)

    def again():
        def step(c, acc):
            x = scores(stream_ref, start_of(c), chunk, bare)
            return jnp.maximum(acc, jnp.max(x, axis=0, keepdims=True))

        exact = rounded(lax.fori_loop(0, m // chunk, step, top))
        return exact + jnp.log2(total(exact))

    return lax.cond(jnp.max(sums) < largest, lambda: shift + jnp.log2(sums), again)


def row_kernel(t_ref, s_ref, out_ref, stream_ref):
    pieces, _, width = t_ref.shape

    @pl.when(pl.program_id(0) == 0)
    def _():
        for k in range(pieces):
            points = t_ref[k, :dim, :]
            lifted = t_ref[k, dim : dim + 1, :].astype(jnp.float32)
            wide = points.astype(jnp.float32)
            bias = scale * (lifted - jnp.sum(wide * wide, axis=0, keepdims=True))
            stream_ref[k * width : (k + 1) * width, :] = streamed_features(points, bias)

    points = jnp.concatenate([s_ref[k, :dim, :] for k in range(s_ref.shape[0])], axis=1)
    out_ref[...] = log_sums(stream_ref, points, 1024, 3)


def column_kernel(s_ref, lse_ref, t_ref, out_ref, stream_ref):
    pieces, _, width = s_ref.shape

    @pl.when(pl.program_id(0) == 0)
    def _():
        for k in range(pieces):
            logw = s_ref[k, dim : dim + 3, :].astype(jnp.float32)
            logw = jnp.sum(logw, axis=0, keepdims=True)
            bias = log2e * logw - lse_ref[:, k * width : (k + 1) * width]
            stream_ref[k * width : (k + 1) * width, :] = streamed_features(s_ref[k, :dim, :], bias)

    points = jnp.concatenate([t_ref[k, :dim, :] for k in range(t_ref.shape[0])], axis=1)
    out_ref[...] = log_sums(stream_ref, points, 1024, 2)


params = dict(
    compiler_params=pltpu.CompilerParams(vmem_limit_bytes=48 * 2**20),
)


def row_sums(targets, sources):
    pieces, height, width = targets.shape
    count, s_height, s_width = sources.shape
    take = 2
    return pl.pallas_call(
        row_kernel,
        grid=(count // take,),
        in_specs=[
            pl.BlockSpec((pieces, height, width), lambda i: (0, 0, 0)),
            pl.BlockSpec((take, s_height, s_width), lambda i: (i, 0, 0)),
        ],
        out_specs=pl.BlockSpec((1, take * s_width), lambda i: (0, i)),
        out_shape=jax.ShapeDtypeStruct((1, count * s_width), jnp.float32),
        scratch_shapes=[pltpu.VMEM((pieces * width, 128), jnp.bfloat16)],
        name="row_sums",
        **params,
    )(targets, sources)


def column_sums(sources, lse, targets):
    pieces, height, width = sources.shape
    count, t_height, t_width = targets.shape
    return pl.pallas_call(
        column_kernel,
        grid=(count,),
        in_specs=[
            pl.BlockSpec((pieces, height, width), lambda i: (0, 0, 0)),
            pl.BlockSpec((1, pieces * width), lambda i: (0, 0)),
            pl.BlockSpec((1, t_height, t_width), lambda i: (i, 0, 0)),
        ],
        out_specs=pl.BlockSpec((1, t_width), lambda i: (0, i)),
        out_shape=jax.ShapeDtypeStruct((1, count * t_width), jnp.float32),
        scratch_shapes=[pltpu.VMEM((pieces * width, 128), jnp.bfloat16)],
        name="column_sums",
        **params,
    )(sources, lse, targets)


def exchange(x, axes, flip):
    size = lax.axis_size(axes)
    return lax.ppermute(x, axes, [(i, i ^ flip) for i in range(size)])


def doubled(x, axes, flip, bit):
    other = exchange(x, axes, flip)
    first = bit == 0
    return jnp.concatenate([jnp.where(first, x, other), jnp.where(first, other, x)], axis=0)


def log_add(a, b):
    top = jnp.maximum(a, b)
    return top + jnp.log2(1.0 + jnp.exp2(-jnp.abs(a - b)))


def norms(points):
    wide = points.astype(jnp.float32)
    return jnp.sum(wide * wide, axis=0)


def per_device(source, target, source_logw, target_logw, start_potential):
    z, y, xh, xl, core = (lax.axis_index(name) for name in names)
    width, span = source.shape[1], target.shape[1]
    own = lax.dynamic_slice_in_dim(source_logw, (2 * xl + core) * width, width, 0)
    first = lax.reduce_precision(own, 8, 7)
    second = lax.reduce_precision(own - first, 8, 7)
    parts = jnp.stack([first, second, own - first - second]).astype(jnp.bfloat16)
    sources = jnp.concatenate([source, parts], axis=0)[None]
    targets = jnp.concatenate([target, start_potential], axis=0)[None]
    x = ("xh", "xl")

    sources = doubled(sources, x, 1, xl)
    targets = doubled(targets, x, 3, xh)
    sources = doubled(sources, "z", 1, z % 2)
    targets = doubled(targets, "y", 1, y % 2)
    sources = doubled(sources, "z", 3, z // 2)
    targets = doubled(targets, "y", 3, y // 2)
    sources = doubled(sources, "core", 1, core)

    lse = row_sums(targets, sources)
    for axes, flip in (("core", 1), (x, 1), ("z", 1), ("z", 3)):
        lse = log_add(lse, exchange(lse, axes, flip))

    partial = column_sums(sources, lse, targets).reshape(2, 2, 2, span)
    for axes, flip, bit in (("y", 3, y // 2), ("y", 1, y % 2), (x, 3, xh)):
        kept = lax.dynamic_index_in_dim(partial, bit, 0, False)
        sent = lax.dynamic_index_in_dim(partial, 1 - bit, 0, False)
        partial = log_add(kept, exchange(sent, axes, flip))

    mine = lax.dynamic_index_in_dim(lse.reshape(2, 4, 2, width), z, 1, False)
    mine = mine.transpose(1, 0, 2).reshape(4 * width)
    picked = lax.dynamic_index_in_dim(
        sources[:, :dim, :].reshape(2, 4, 2, dim, width), z, 1, False
    )
    row_sq = jnp.sum(jnp.square(picked.astype(jnp.float32)), axis=2)
    row_sq = row_sq.transpose(1, 0, 2).reshape(4 * width)
    row_lse = mine / log2e - row_sq / smoothing
    row_potential = smoothing * source_logw - smoothing * row_lse

    col_lse = partial / log2e - norms(target) / smoothing
    col_potential = smoothing * target_logw - smoothing * col_lse
    return (row_potential, col_potential)


def solution(mesh):
    devices = Mesh(mesh.devices.reshape(shape), names)
    rows = ("z", "y", "xh")
    columns = ("xl", "core", "z", "y", "xh")
    in_specs = (P(None, names), P(None, columns), P(rows), P(columns), P(None, columns))
    out_specs = (P(rows), P(columns))
    return jax.shard_map(
        per_device, mesh=devices, in_specs=in_specs, out_specs=out_specs, check_vma=False
    )
```

time: 538 us -> 115 us (0.21)
  waiting for transfers between devices: 146 us -> 30 us
  blocking collectives: 109 us -> 0 us
  other arithmetic: 101 us -> 4.37 us
  matrix products: 73.6 us -> 0 us
  local copies, waits for them, and re-layouts: 71.1 us -> 0.64 us
  starting transfers between devices: 0.3 us -> 41.8 us
  Pallas kernels: 0 us -> 37.7 us
  loops' own time: 18.1 us -> 0 us
  between operations: 13.9 us -> 0.93 us
    all_gather x3 -> x0, waiting for transfers between devices: 146 us -> none  [the longest x2 145 us: combined_all(): gathered = jax.tree.map(lambda a: lax.all_gather(a, axis), part)]
    all_gather x4 -> x0, blocking collectives: 109 us -> none  [the longest x1 93.3 us: per_device(): lax.all_gather(start_potential, 'row', axis=1, tiled=True)]
    reduce_sum x49 -> x2, other arithmetic: 97.5 us -> 0.08 us  [the longest x1 0.05 us: per_device(): row_sq = jnp.sum(jnp.square(picked.astype(jnp.float32)), axis=2)]
    dot_general x24 -> x0, matrix products: 73.6 us -> none  [cost_block(): lax.dot_general(rows, cols, (((0,), (0,)), ((), ())), preferred_element_t...]
    dynamic_slice x63 -> x1, local copies, waits for them, and re-layouts: 55.5 us -> 0.03 us  [per_device(): sent = lax.dynamic_index_in_dim(partial, 1 - bit, 0, False)]
    ppermute x0 -> x14, starting transfers between devices: none -> 41.8 us  [exchange(): return lax.ppermute(x, axes, [(i, i ^ flip) for i in range(size)])]
    pallas_call x0 -> x2, Pallas kernels: none -> 37.7 us  [the longest x1 18.9 us: column_sums(): pl.pallas_call(column_kernel, grid=(count,), in_specs=[pl.BlockSpec((piec...]
    ppermute x0 -> x14, waiting for transfers between devices: none -> 30 us  [exchange(): return lax.ppermute(x, axes, [(i, i ^ flip) for i in range(size)])]
  transfers between devices with their start and end apart: 3 -> 14, of which waited for: 2 -> 11; matrix products, arithmetic and copies ran while one was open for 1% -> 1% of each run, Pallas kernels for 0% -> 0%
where the time goes in v1:
time: 115 us
  starting transfers between devices  41.8 us (36%)
  Pallas kernels  37.7 us (33%)
  waiting for transfers between devices  30 us (26%)
  other arithmetic  4.37 us (4%)
    ppermute x14, starting transfers between devices, exchange(): return lax.ppermute(x, axes, [(i, i ^ flip) for i in range(size)])  41.8 us
    ppermute x14, waiting for transfers between devices, exchange(): return lax.ppermute(x, axes, [(i, i ^ flip) for i in range(size)])  30 us
    pallas_call x1, Pallas kernels, column_sums(): pl.pallas_call(column_kernel, grid=(count,), in_specs=[pl.BlockSpec((piec...  18.9 us
    pallas_call x1, Pallas kernels, row_sums(): pl.pallas_call(row_kernel, grid=(count // take,), in_specs=[pl.BlockSpec(...  18.8 us
  transfers between devices with their start and end apart: 14, of which 11 were waited for; matrix products, arithmetic and copies ran while one was open for 1% of the time, Pallas kernels for 0%

profile of v1, /device:TPU:8, one launch (start us, length us, event | category | flops | bytes accessed | tf_op | source)
XLA Modules:
  0.0 115.5 jit_solution(6741961298706000637)
XLA Ops:
  0.6 0.0 copy-start.1
  0.6 0.8 reduce-precision_convert_fusion.1
  1.4 0.0 copy-done.1
  1.5 1.6 %collective-permute-start.3 = (bf16[1,67,256]{2,1,0:T(8,128)(2,1)S(1)}, bf16[1,67,256]{2,1,0:T(8,128)(2,1)S(1)}, u32[]{:S(2)}, u32[]{:S(2)}) collective-permute-start(bf16[1,67,256]{2,1,0:T(8,128)(2,1)S(1)} %maximum_bitcast_fusion.1), channel_id=1, source_target_pairs={{0,2},{2,0},{4,6},{6,4},{1,3},{3,1},{5,7},{7,5},{8,10},{10,8},{12,... | collective-permute-start | bytes 102920 | tf_op jit(solution)/shard_map/ppermute | solution.py:172
  3.0 2.5 %collective-permute-done.3 = bf16[1,67,256]{2,1,0:T(8,128)(2,1)S(1)} collective-permute-done((bf16[1,67,256]{2,1,0:T(8,128)(2,1)S(1)}, bf16[1,67,256]{2,1,0:T(8,128)(2,1)S(1)}, u32[]{:S(2)}, u32[]{:S(2)}) %collective-permute-start.3) | collective-permute-done | bytes 34336 | tf_op jit(solution)/shard_map/ppermute | solution.py:172
  5.5 0.0 copy-start
  5.5 0.0 copy-start.2
  5.6 2.0 %collective-permute-start.4 = (bf16[2,67,256]{2,1,0:T(8,128)(2,1)S(1)}, bf16[2,67,256]{2,1,0:T(8,128)(2,1)S(1)}, u32[]{:S(2)}, u32[]{:S(2)}) collective-permute-start(bf16[2,67,256]{2,1,0:T(8,128)(2,1)S(1)} %pad_maximum_fusion.6), channel_id=1, source_target_pairs={{0,32},{32,0},{64,96},{96,64},{1,33},{33,1},{65,97},{97,65},{2,34}... | collective-permute-start | bytes 205832 | tf_op jit(solution)/shard_map/ppermute | solution.py:172
  7.6 0.0 copy-done
  7.6 2.8 %collective-permute-start = (bf16[1,65,768]{2,1,0:T(8,128)(2,1)S(1)}, bf16[1,65,768]{2,1,0:T(8,128)(2,1)S(1)}, u32[]{:S(2)}, u32[]{:S(2)}) collective-permute-start(bf16[1,65,768]{2,1,0:T(8,128)(2,1)S(1)} %maximum_bitcast_fusion), channel_id=1, source_target_pairs={{0,6},{2,4},{4,2},{6,0},{1,7},{3,5},{5,3},{7,1},{8,14},{10,12},{12... | collective-permute-start | bytes 299528 | tf_op jit(solution)/shard_map/ppermute | solution.py:172
  10.4 0.0 collective-permute-done.4
  10.5 3.7 %collective-permute-start.5 = (bf16[4,67,256]{2,1,0:T(8,128)(2,1)S(1)}, bf16[4,67,256]{2,1,0:T(8,128)(2,1)S(1)}, u32[]{:S(2)}, u32[]{:S(2)}) collective-permute-start(bf16[4,67,256]{2,1,0:T(8,128)(2,1)S(1)} %pad_maximum_fusion.5), channel_id=1, source_target_pairs={{0,96},{32,64},{64,32},{96,0},{1,97},{33,65},{65,33},{97,1},{2,98}... | collective-permute-start | bytes 411656 | tf_op jit(solution)/shard_map/ppermute | solution.py:172
  14.2 0.0 collective-permute-done
  14.3 0.5 collective-permute-start.1
  14.8 2.5 %collective-permute-done.5 = bf16[4,67,256]{2,1,0:T(8,128)(2,1)S(1)} collective-permute-done((bf16[4,67,256]{2,1,0:T(8,128)(2,1)S(1)}, bf16[4,67,256]{2,1,0:T(8,128)(2,1)S(1)}, u32[]{:S(2)}, u32[]{:S(2)}) %collective-permute-start.5) | collective-permute-done | bytes 137248 | tf_op jit(solution)/shard_map/ppermute | solution.py:172
  17.4 0.1 collective-permute-start.6
  17.5 2.8 %collective-permute-done.1 = bf16[2,65,768]{2,1,0:T(8,128)(2,1)S(1)} collective-permute-done((bf16[2,65,768]{2,1,0:T(8,128)(2,1)S(1)}, bf16[2,65,768]{2,1,0:T(8,128)(2,1)S(1)}, u32[]{:S(2)}, u32[]{:S(2)}) %collective-permute-start.1) | collective-permute-done | bytes 199712 | tf_op jit(solution)/shard_map/ppermute | solution.py:172
  20.4 1.7 %collective-permute-start.2 = (bf16[4,65,768]{2,1,0:T(8,128)(2,1)S(1)}, bf16[4,65,768]{2,1,0:T(8,128)(2,1)S(1)}, u32[]{:S(2)}, u32[]{:S(2)}) collective-permute-start(bf16[4,65,768]{2,1,0:T(8,128)(2,1)S(1)} %pad_maximum_fusion.2), channel_id=1, source_target_pairs={{0,24},{8,16},{16,8},{24,0},{1,25},{9,17},{17,9},{25,1},{2,26},{10... | collective-permute-start | bytes 1198088 | tf_op jit(solution)/shard_map/ppermute | solution.py:172
  22.0 0.0 collective-permute-done.6
  22.1 0.1 pad_maximum_fusion.1.s_ref
  22.1 8.1 %collective-permute-done.2 = bf16[4,65,768]{2,1,0:T(8,128)(2,1)S(1)} collective-permute-done((bf16[4,65,768]{2,1,0:T(8,128)(2,1)S(1)}, bf16[4,65,768]{2,1,0:T(8,128)(2,1)S(1)}, u32[]{:S(2)}, u32[]{:S(2)}) %collective-permute-start.2) | collective-permute-done | bytes 399392 | tf_op jit(solution)/shard_map/ppermute | solution.py:172
  30.2 0.1 broadcast_select_fusion.1
  30.3 0.1 pad_maximum_fusion.t_ref
  30.4 18.8 %row_sums.1 = f32[1,4096]{1,0:T(1,128)S(1)} custom-call(bf16[8,65,768]{2,1,0:T(8,128)(2,1)S(1)} %pad_maximum_fusion.t_ref, bf16[16,67,256]{2,1,0:T(8,128)(2,1)S(1)} %pad_maximum_fusion.1.s_ref), custom_call_target="tpu_custom_call" | custom-call | tf_op jit(solution)/shard_map/row_sums/pallas_call | solution.py:136
  49.2 0.1 collective-permute-start.7
  49.3 1.2 %collective-permute-done.7 = f32[1,4096]{1,0:T(1,128)S(1)} collective-permute-done((f32[1,4096]{1,0:T(1,128)S(1)}, f32[1,4096]{1,0:T(1,128)S(1)}, u32[]{:S(2)}, u32[]{:S(2)}) %collective-permute-start.7) | collective-permute-done | bytes 16416 | tf_op jit(solution)/shard_map/ppermute | solution.py:172
  50.4 0.1 multiply_add_fusion.3
  50.5 1.6 %collective-permute-start.8 = (f32[1,4096]{1,0:T(1,128)S(1)}, f32[1,4096]{1,0:T(1,128)S(1)}, u32[]{:S(2)}, u32[]{:S(2)}) collective-permute-start(f32[1,4096]{1,0:T(1,128)S(1)} %multiply_add_fusion.3), channel_id=1, source_target_pairs={{0,2},{2,0},{4,6},{6,4},{1,3},{3,1},{5,7},{7,5},{8,10},{10,8},{12,... | collective-permute-start | bytes 49160 | tf_op jit(solution)/shard_map/ppermute | solution.py:172
  52.1 2.2 %collective-permute-done.8 = f32[1,4096]{1,0:T(1,128)S(1)} collective-permute-done((f32[1,4096]{1,0:T(1,128)S(1)}, f32[1,4096]{1,0:T(1,128)S(1)}, u32[]{:S(2)}, u32[]{:S(2)}) %collective-permute-start.8) | collective-permute-done | bytes 16416 | tf_op jit(solution)/shard_map/ppermute | solution.py:172
  54.3 0.1 multiply_add_fusion.2
  54.4 8.6 %collective-permute-start.9 = (f32[1,4096]{1,0:T(1,128)S(1)}, f32[1,4096]{1,0:T(1,128)S(1)}, u32[]{:S(2)}, u32[]{:S(2)}) collective-permute-start(f32[1,4096]{1,0:T(1,128)S(1)} %multiply_add_fusion.2), channel_id=1, source_target_pairs={{0,32},{32,0},{64,96},{96,64},{1,33},{33,1},{65,97},{97,65},{2,34}... | collective-permute-start | bytes 49160 | tf_op jit(solution)/shard_map/ppermute | solution.py:172
  63.0 1.7 %collective-permute-done.9 = f32[1,4096]{1,0:T(1,128)S(1)} collective-permute-done((f32[1,4096]{1,0:T(1,128)S(1)}, f32[1,4096]{1,0:T(1,128)S(1)}, u32[]{:S(2)}, u32[]{:S(2)}) %collective-permute-start.9) | collective-permute-done | bytes 16416 | tf_op jit(solution)/shard_map/ppermute | solution.py:172
  64.7 0.1 multiply_add_fusion.1
  64.8 6.0 %collective-permute-start.10 = (f32[1,4096]{1,0:T(1,128)S(1)}, f32[1,4096]{1,0:T(1,128)S(1)}, u32[]{:S(2)}, u32[]{:S(2)}) collective-permute-start(f32[1,4096]{1,0:T(1,128)S(1)} %multiply_add_fusion.1), channel_id=1, source_target_pairs={{0,96},{32,64},{64,32},{96,0},{1,97},{33,65},{65,33},{97,1},{2,98}... | collective-permute-start | bytes 49160 | tf_op jit(solution)/shard_map/ppermute | solution.py:172
  70.8 1.7 %collective-permute-done.10 = f32[1,4096]{1,0:T(1,128)S(1)} collective-permute-done((f32[1,4096]{1,0:T(1,128)S(1)}, f32[1,4096]{1,0:T(1,128)S(1)}, u32[]{:S(2)}, u32[]{:S(2)}) %collective-permute-start.10) | collective-permute-done | bytes 16416 | tf_op jit(solution)/shard_map/ppermute | solution.py:172
  72.5 0.5 broadcast.81
  73.0 0.7 fusion.16
  73.7 18.9 %column_sums.1 = f32[1,6144]{1,0:T(1,128)S(1)} custom-call(bf16[16,67,256]{2,1,0:T(8,128)(2,1)S(1)} %pad_maximum_fusion.1.s_ref, f32[1,4096]{1,0:T(1,128)S(1)} %get-tuple-element.5.lse_ref, bf16[8,65,768]{2,1,0:T(8,128)(2,1)S(1)} %pad_maximum_fusion.t_ref), custom_call_target="tpu_custom_call" | custom-call | tf_op jit(solution)/shard_map/column_sums/pallas_call | solution.py:154
  92.6 0.7 reduce.12
  93.4 1.1 collective-permute-start.11
  94.6 2.5 %collective-permute-done.11 = f32[2,2,768]{2,1,0:T(2,128)S(1)} collective-permute-done((f32[2,2,768]{2,1,0:T(2,128)S(1)}, f32[2,2,768]{2,1,0:T(2,128)S(1)}, u32[]{:S(2)}, u32[]{:S(2)}) %collective-permute-start.11) | collective-permute-done | bytes 12320 | tf_op jit(solution)/shard_map/ppermute | solution.py:172
  97.2 11.1 %collective-permute-start.12 = (f32[2,768]{1,0:T(2,128)S(1)}, f32[2,768]{1,0:T(2,128)S(1)}, u32[]{:S(2)}, u32[]{:S(2)}) collective-permute-start(f32[2,768]{1,0:T(2,128)S(1)} %dynamic-slice_bitcast_fusion.1), channel_id=1, source_target_pairs={{0,8},{8,0},{16,24},{24,16},{1,9},{9,1},{17,25},{25,17},{2,10},{10... | collective-permute-start | bytes 18440 | tf_op jit(solution)/shard_map/ppermute | solution.py:172
  108.3 1.6 %collective-permute-done.12 = f32[2,768]{1,0:T(2,128)S(1)} collective-permute-done((f32[2,768]{1,0:T(2,128)S(1)}, f32[2,768]{1,0:T(2,128)S(1)}, u32[]{:S(2)}, u32[]{:S(2)}) %collective-permute-start.12) | collective-permute-done | bytes 6176 | tf_op jit(solution)/shard_map/ppermute | solution.py:172
  109.9 0.0 copy-start.3
  110.0 1.1 collective-permute-start.13
  111.0 0.6 multiply_subtract_fusion.1
  111.6 3.2 %collective-permute-done.13 = f32[768]{0:T(1024)S(1)} collective-permute-done((f32[768]{0:T(1024)S(1)}, f32[768]{0:T(1024)S(1)}, u32[]{:S(2)}, u32[]{:S(2)}) %collective-permute-start.13) | collective-permute-done | bytes 3104 | tf_op jit(solution)/shard_map/ppermute | solution.py:172
  114.9 0.6 multiply_subtract_fusion
  (33 shorter events, 0.7 us)
Async XLA Ops:
  0.6 0.8 copy-start.1
  1.5 4.0 %collective-permute-start.3 = (bf16[1,67,256]{2,1,0:T(8,128)(2,1)S(1)}, bf16[1,67,256]{2,1,0:T(8,128)(2,1)S(1)}, u32[]{:S(2)}, u32[]{:S(2)}) collective-permute-start(bf16[1,67,256]{2,1,0:T(8,128)(2,1)S(1)} %maximum_bitcast_fusion.1), channel_id=1, source_target_pairs={{0,2},{2,0},{4,6},{6,4},{1,3},{3,1},{5,7},{7,5},{8,10},{10,8},{12,... | collective-permute-start | bytes 102920 | tf_op jit(solution)/shard_map/ppermute | solution.py:172
  5.5 2.0 %copy-start = (bf16[64,768]{1,0:T(8,128)(2,1)S(1)}, bf16[64,768]{1,0:T(8,128)(2,1)}, u32[]{:S(2)}) copy-start(bf16[64,768]{1,0:T(8,128)(2,1)} %param.6) | copy-start | bytes 294916
  5.5 2.0 %copy-start.2 = (bf16[1,768]{1,0:T(2,128)(2,1)S(1)}, bf16[1,768]{1,0:T(2,128)(2,1)}, u32[]{:S(2)}) copy-start(bf16[1,768]{1,0:T(2,128)(2,1)} %param.9) | copy-start | bytes 4612
  5.6 4.9 %collective-permute-start.4 = (bf16[2,67,256]{2,1,0:T(8,128)(2,1)S(1)}, bf16[2,67,256]{2,1,0:T(8,128)(2,1)S(1)}, u32[]{:S(2)}, u32[]{:S(2)}) collective-permute-start(bf16[2,67,256]{2,1,0:T(8,128)(2,1)S(1)} %pad_maximum_fusion.6), channel_id=1, source_target_pairs={{0,32},{32,0},{64,96},{96,64},{1,33},{33,1},{65,97},{97,65},{2,34}... | collective-permute-start | bytes 205832 | tf_op jit(solution)/shard_map/ppermute | solution.py:172
  7.6 6.6 %collective-permute-start = (bf16[1,65,768]{2,1,0:T(8,128)(2,1)S(1)}, bf16[1,65,768]{2,1,0:T(8,128)(2,1)S(1)}, u32[]{:S(2)}, u32[]{:S(2)}) collective-permute-start(bf16[1,65,768]{2,1,0:T(8,128)(2,1)S(1)} %maximum_bitcast_fusion), channel_id=1, source_target_pairs={{0,6},{2,4},{4,2},{6,0},{1,7},{3,5},{5,3},{7,1},{8,14},{10,12},{12... | collective-permute-start | bytes 299528 | tf_op jit(solution)/shard_map/ppermute | solution.py:172
  10.5 6.8 %collective-permute-start.5 = (bf16[4,67,256]{2,1,0:T(8,128)(2,1)S(1)}, bf16[4,67,256]{2,1,0:T(8,128)(2,1)S(1)}, u32[]{:S(2)}, u32[]{:S(2)}) collective-permute-start(bf16[4,67,256]{2,1,0:T(8,128)(2,1)S(1)} %pad_maximum_fusion.5), channel_id=1, source_target_pairs={{0,96},{32,64},{64,32},{96,0},{1,97},{33,65},{65,33},{97,1},{2,98}... | collective-permute-start | bytes 411656 | tf_op jit(solution)/shard_map/ppermute | solution.py:172
  14.3 6.0 %collective-permute-start.1 = (bf16[2,65,768]{2,1,0:T(8,128)(2,1)S(1)}, bf16[2,65,768]{2,1,0:T(8,128)(2,1)S(1)}, u32[]{:S(2)}, u32[]{:S(2)}) collective-permute-start(bf16[2,65,768]{2,1,0:T(8,128)(2,1)S(1)} %pad_maximum_fusion.4), channel_id=1, source_target_pairs={{0,8},{8,0},{16,24},{24,16},{1,9},{9,1},{17,25},{25,17},{2,10},{10... | collective-permute-start | bytes 599048 | tf_op jit(solution)/shard_map/ppermute | solution.py:172
  17.4 4.7 %collective-permute-start.6 = (bf16[8,67,256]{2,1,0:T(8,128)(2,1)S(1)}, bf16[8,67,256]{2,1,0:T(8,128)(2,1)S(1)}, u32[]{:S(2)}, u32[]{:S(2)}) collective-permute-start(bf16[8,67,256]{2,1,0:T(8,128)(2,1)S(1)} %pad_maximum_fusion.3), channel_id=1, source_target_pairs={{0,1},{1,0},{2,3},{3,2},{4,5},{5,4},{6,7},{7,6},{8,9},{9,8},{10,11... | collective-permute-start | bytes 823304 | tf_op jit(solution)/shard_map/ppermute | solution.py:172
  20.4 9.8 %collective-permute-start.2 = (bf16[4,65,768]{2,1,0:T(8,128)(2,1)S(1)}, bf16[4,65,768]{2,1,0:T(8,128)(2,1)S(1)}, u32[]{:S(2)}, u32[]{:S(2)}) collective-permute-start(bf16[4,65,768]{2,1,0:T(8,128)(2,1)S(1)} %pad_maximum_fusion.2), channel_id=1, source_target_pairs={{0,24},{8,16},{16,8},{24,0},{1,25},{9,17},{17,9},{25,1},{2,26},{10... | collective-permute-start | bytes 1198088 | tf_op jit(solution)/shard_map/ppermute | solution.py:172
  49.2 1.3 %collective-permute-start.7 = (f32[1,4096]{1,0:T(1,128)S(1)}, f32[1,4096]{1,0:T(1,128)S(1)}, u32[]{:S(2)}, u32[]{:S(2)}) collective-permute-start(f32[1,4096]{1,0:T(1,128)S(1)} %row_sums.1), channel_id=1, source_target_pairs={{0,1},{1,0},{2,3},{3,2},{4,5},{5,4},{6,7},{7,6},{8,9},{9,8},{10,11... | collective-permute-start | bytes 49160 | tf_op jit(solution)/shard_map/ppermute | solution.py:172
  50.5 3.8 %collective-permute-start.8 = (f32[1,4096]{1,0:T(1,128)S(1)}, f32[1,4096]{1,0:T(1,128)S(1)}, u32[]{:S(2)}, u32[]{:S(2)}) collective-permute-start(f32[1,4096]{1,0:T(1,128)S(1)} %multiply_add_fusion.3), channel_id=1, source_target_pairs={{0,2},{2,0},{4,6},{6,4},{1,3},{3,1},{5,7},{7,5},{8,10},{10,8},{12,... | collective-permute-start | bytes 49160 | tf_op jit(solution)/shard_map/ppermute | solution.py:172
  54.4 10.3 %collective-permute-start.9 = (f32[1,4096]{1,0:T(1,128)S(1)}, f32[1,4096]{1,0:T(1,128)S(1)}, u32[]{:S(2)}, u32[]{:S(2)}) collective-permute-start(f32[1,4096]{1,0:T(1,128)S(1)} %multiply_add_fusion.2), channel_id=1, source_target_pairs={{0,32},{32,0},{64,96},{96,64},{1,33},{33,1},{65,97},{97,65},{2,34}... | collective-permute-start | bytes 49160 | tf_op jit(solution)/shard_map/ppermute | solution.py:172
  64.8 7.7 %collective-permute-start.10 = (f32[1,4096]{1,0:T(1,128)S(1)}, f32[1,4096]{1,0:T(1,128)S(1)}, u32[]{:S(2)}, u32[]{:S(2)}) collective-permute-start(f32[1,4096]{1,0:T(1,128)S(1)} %multiply_add_fusion.1), channel_id=1, source_target_pairs={{0,96},{32,64},{64,32},{96,0},{1,97},{33,65},{65,33},{97,1},{2,98}... | collective-permute-start | bytes 49160 | tf_op jit(solution)/shard_map/ppermute | solution.py:172
  93.4 3.8 %collective-permute-start.11 = (f32[2,2,768]{2,1,0:T(2,128)S(1)}, f32[2,2,768]{2,1,0:T(2,128)S(1)}, u32[]{:S(2)}, u32[]{:S(2)}) collective-permute-start(f32[2,2,768]{2,1,0:T(2,128)S(1)} %dynamic-slice_bitcast_fusion), channel_id=1, source_target_pairs={{0,24},{8,16},{16,8},{24,0},{1,25},{9,17},{17,9},{25,1},{2,26},{10... | collective-permute-start | bytes 36872 | tf_op jit(solution)/shard_map/ppermute | solution.py:172
  97.2 12.7 %collective-permute-start.12 = (f32[2,768]{1,0:T(2,128)S(1)}, f32[2,768]{1,0:T(2,128)S(1)}, u32[]{:S(2)}, u32[]{:S(2)}) collective-permute-start(f32[2,768]{1,0:T(2,128)S(1)} %dynamic-slice_bitcast_fusion.1), channel_id=1, source_target_pairs={{0,8},{8,0},{16,24},{24,16},{1,9},{9,1},{17,25},{25,17},{2,10},{10... | collective-permute-start | bytes 18440 | tf_op jit(solution)/shard_map/ppermute | solution.py:172
  109.9 1.1 copy-start.3
  110.0 4.9 %collective-permute-start.13 = (f32[768]{0:T(1024)S(1)}, f32[768]{0:T(1024)S(1)}, u32[]{:S(2)}, u32[]{:S(2)}) collective-permute-start(f32[768]{0:T(1024)S(1)} %get-tuple-element.2), channel_id=1, source_target_pairs={{0,6},{2,4},{4,2},{6,0},{1,7},{3,5},{5,3},{7,1},{8,14},{10,12},{12... | collective-permute-start | bytes 9224 | tf_op jit(solution)/shard_map/ppermute | solution.py:172
  111.0 3.8 %copy-start.4 = (f32[768]{0:T(1024)S(1)}, f32[768]{0:T(1024)}, u32[]{:S(2)}) copy-start(f32[768]{0:T(1024)} %param.8) | copy-start | bytes 9220
